TPU v7x, 32 devices: a whole 2x2x4 slice. The times are simulated.
32 devices in a mesh: dp: 8 (over y, x, core), tensor: 4 (over z).
Axes of the slice: x: 2, y: 2, z: 4, core: 2. Of those that a mesh axis runs over, the one named last changes fastest.
Arguments:
- inputs: bfloat16 [2048, 1024], P(('dp', 'tensor')), may hold values from -6 to 6
- first_gain: float32 [1024], replicated, may hold values from 0.1 to 1.9
- entry_projection_weight: bfloat16 [3, 1024, 1024], P(None, 'dp', 'tensor'), may hold values from -0.1875 to 0.1875
- conv_weight: float32 [3, 1024], replicated, may hold values from -3 to 3
- out_weight: bfloat16 [1024, 1024], P('tensor', 'dp'), may hold values from -0.1875 to 0.1875
- second_gain: float32 [1024], replicated, may hold values from 0.1 to 1.9
- gate_up_weight: bfloat16 [2, 1024, 4608], P(None, 'dp', 'tensor'), may hold values from -0.1875 to 0.1875
- down_weight: bfloat16 [4608, 1024], P('tensor', 'dp'), may hold values from -0.09375 to 0.09375
- cotangent: bfloat16 [2048, 1024], P(('dp', 'tensor')), may hold values from -6 to 6
- lengths: int32 [4], replicated, may hold values from 1 to 1024, 2048 in all
Outputs:
- output: bfloat16 [2048, 1024], P(('dp', 'tensor'))
- input_grad: float32 [2048, 1024], P(('dp', 'tensor'))
- first_gain_grad: float32 [1024], replicated
- in_weight_grad: float32 [3, 1024, 1024], P(None, 'dp', 'tensor')
- filter_weight_gradient: float32 [3, 1024], replicated
- out_weight_grad: float32 [1024, 1024], P('tensor', 'dp')
- second_gain_grad: float32 [1024], replicated
- gate_up_grad: float32 [2, 1024, 4608], P(None, 'dp', 'tensor')
- down_grad: float32 [4608, 1024], P('tensor', 'dp')
Inputs may be any that keep to these rules, and one draw needn't show every extreme that they name: lengths of the 4 sequences packed end to end in token order; they sum to 2048, and the longest is exactly 1024.
All inputs are finite; a program needn't handle non-finite values.
Results may differ from a plain program's by a relative error of at most 0.012.
Values may be sent and summed in bfloat16 or wider, within the bound.
A program may use at most 128 MiB of HBM per device.

v0:
```python
import jax
import jax.numpy as jnp
from jax import lax
from jax.sharding import PartitionSpec as P

EPS = 1e-05


def passed_along(block, axis, distance):
    devices = range(lax.axis_size(axis))
    route = [(i - distance, i) for i in devices if i - distance in devices]
    return lax.ppermute(block, axis, route)


def rms_norm(values, gain):
    return values * lax.rsqrt(jnp.mean(values * values, axis=-1, keepdims=True) + EPS) * gain


def rms_back(values, gain, grad_out):
    scale = lax.rsqrt(jnp.mean(values * values, axis=-1, keepdims=True) + EPS)
    normal = values * scale
    weighted = gain * grad_out
    grad_in = scale * (weighted - normal * jnp.mean(normal * weighted, axis=-1, keepdims=True))
    return (grad_in, jnp.sum(normal * grad_out, axis=0))


def times_trans(left, right):
    return lax.dot_general(
        left, right, (((1,), (1,)), ((), ())), preferred_element_type=jnp.float32
    )


def trans_times(left, right):
    return lax.dot_general(
        left, right, (((0,), (0,)), ((), ())), preferred_element_type=jnp.float32
    )


def shards(
    inputs,
    first_gain,
    entry_projection_weight,
    conv_weight,
    out_weight,
    second_gain,
    gate_up_weight,
    down_weight,
    cotangent,
    lengths,
):
    own_rows = inputs.shape[0]
    group_rows = own_rows * lax.axis_size("tensor")
    channels = entry_projection_weight.shape[2]
    column = lax.axis_index("tensor") * channels
    start = lax.axis_index("dp") * group_rows
    ends = jnp.cumsum(lengths)
    places = start - 2 + jnp.arange(group_rows + 4, dtype=jnp.int32)
    segment = jnp.sum((places[:, None] >= ends[None, :]).astype(jnp.int32), axis=1)
    first_all = jnp.logical_and(segment[2:] == segment[1:-1], places[2:] >= 1).astype(jnp.float32)[
        :, None
    ]
    second_all = jnp.logical_and(segment[2:] == segment[:-2], places[2:] >= 2).astype(jnp.float32)[
        :, None
    ]
    first_keep = first_all[:group_rows]
    second_keep = second_all[:group_rows]
    kernel = lax.dynamic_slice_in_dim(conv_weight, column, channels, 1)
    residual = inputs.astype(jnp.float32)
    normed = lax.all_gather(
        rms_norm(residual, first_gain).astype(jnp.bfloat16), "tensor", axis=0, tiled=True
    )
    in_full, out_full, gate_up_full, down_full = (
        lax.all_gather(entry_projection_weight, "dp", axis=1, tiled=True),
        lax.all_gather(out_weight, "dp", axis=1, tiled=True),
        lax.all_gather(gate_up_weight, "dp", axis=1, tiled=True),
        lax.all_gather(down_weight, "dp", axis=1, tiled=True),
    )
    projected = jnp.einsum("td,kdc->ktc", normed, in_full, preferred_element_type=jnp.float32)
    input_gate_value = projected[0]
    c_value = projected[1]
    v_value = projected[2]
    product = (input_gate_value * v_value).astype(jnp.bfloat16)
    before = passed_along(product[-2:], "dp", 1)
    extended = jnp.concatenate([before, product], axis=0).astype(jnp.float32)
    mixed = (
        kernel[2] * extended[2:]
        + kernel[1] * first_keep * extended[1:-1]
        + kernel[0] * second_keep * extended[:-2]
    )
    gated = (c_value * mixed).astype(jnp.bfloat16)
    mixer_part = jnp.dot(gated, out_full, preferred_element_type=jnp.float32)
    middle = residual + lax.psum_scatter(mixer_part, "tensor", scatter_dimension=0, tiled=True)
    hidden_in = lax.all_gather(
        rms_norm(middle, second_gain).astype(jnp.bfloat16), "tensor", axis=0, tiled=True
    )
    gate_up = jnp.einsum("td,kdf->ktf", hidden_in, gate_up_full, preferred_element_type=jnp.float32)
    gate_value = gate_up[0]
    up_value = gate_up[1]
    sigmoid = jax.nn.sigmoid(gate_value)
    swish = gate_value * sigmoid
    hidden = (swish * up_value).astype(jnp.bfloat16)
    ffn_part = jnp.dot(hidden, down_full, preferred_element_type=jnp.float32)
    output = (
        middle
        + lax.psum_scatter(
            ffn_part.astype(jnp.bfloat16), "tensor", scatter_dimension=0, tiled=True
        ).astype(jnp.float32)
    ).astype(jnp.bfloat16)
    in_full, out_full, gate_up_full, down_full = (
        lax.all_gather(entry_projection_weight, "dp", axis=1, tiled=True),
        lax.all_gather(out_weight, "dp", axis=1, tiled=True),
        lax.all_gather(gate_up_weight, "dp", axis=1, tiled=True),
        lax.all_gather(down_weight, "dp", axis=1, tiled=True),
    )
    grad_rows = lax.all_gather(cotangent, "tensor", axis=0, tiled=True)
    grad_hidden = times_trans(grad_rows, down_full)
    down_part = trans_times(hidden, grad_rows)
    grad_gate = (grad_hidden * up_value * sigmoid * (1.0 + gate_value * (1.0 - sigmoid))).astype(
        jnp.bfloat16
    )
    grad_up = (grad_hidden * swish).astype(jnp.bfloat16)
    gate_up_stack = jnp.stack([grad_gate, grad_up])
    gate_up_part = jnp.einsum(
        "td,ktf->kdf", hidden_in, gate_up_stack, preferred_element_type=jnp.float32
    )
    hidden_back = jnp.einsum(
        "ktf,kdf->td", gate_up_stack, gate_up_full, preferred_element_type=jnp.float32
    )
    grad_hin = lax.psum_scatter(hidden_back, "tensor", scatter_dimension=0, tiled=True)
    second_back, second_part = rms_back(middle, second_gain, grad_hin)
    grad_middle = cotangent.astype(jnp.float32) + second_back
    branch_rows = lax.all_gather(grad_middle.astype(jnp.bfloat16), "tensor", axis=0, tiled=True)
    grad_gated = times_trans(branch_rows, out_full)
    out_part = trans_times(gated, branch_rows)
    output_gate_gradient = (grad_gated * mixed).astype(jnp.bfloat16)
    grad_mixed = (grad_gated * c_value).astype(jnp.bfloat16)
    after = passed_along(grad_mixed[:2], "dp", -1)
    grad_ext = jnp.concatenate([grad_mixed, after], axis=0).astype(jnp.float32)
    mixed_wide = grad_ext[:-2]
    kernel_part = jnp.stack(
        [
            jnp.sum(second_keep * extended[:-2] * mixed_wide, axis=0),
            jnp.sum(first_keep * extended[1:-1] * mixed_wide, axis=0),
            jnp.sum(extended[2:] * mixed_wide, axis=0),
        ]
    )
    kernel_full = lax.dynamic_update_slice_in_dim(
        jnp.zeros(conv_weight.shape, jnp.float32), kernel_part, column, 1
    )
    elementwise_product_gradient = (
        kernel[2] * grad_ext[:-2]
        + kernel[1] * first_all[1:-1] * grad_ext[1:-1]
        + kernel[0] * second_all[2:] * grad_ext[2:]
    )
    input_gate_gradient = (elementwise_product_gradient * v_value).astype(jnp.bfloat16)
    value_branch_gradient = (elementwise_product_gradient * input_gate_value).astype(jnp.bfloat16)
    stacked_projection_outputs = jnp.stack(
        [input_gate_gradient, output_gate_gradient, value_branch_gradient]
    )
    in_part = jnp.einsum(
        "td,ktc->kdc", normed, stacked_projection_outputs, preferred_element_type=jnp.float32
    )
    normed_back = jnp.einsum(
        "ktc,kdc->td", stacked_projection_outputs, in_full, preferred_element_type=jnp.float32
    )
    grad_normed = lax.psum_scatter(
        normed_back.astype(jnp.bfloat16), "tensor", scatter_dimension=0, tiled=True
    ).astype(jnp.float32)
    first_back, first_part = rms_back(residual, first_gain, grad_normed)
    input_grad = grad_middle + first_back
    in_grad, out_grad, gate_up_grad, down_grad = (
        lax.psum_scatter(in_part, "dp", scatter_dimension=1, tiled=True),
        lax.psum_scatter(out_part, "dp", scatter_dimension=1, tiled=True),
        lax.psum_scatter(gate_up_part, "dp", scatter_dimension=1, tiled=True),
        lax.psum_scatter(down_part, "dp", scatter_dimension=1, tiled=True),
    )
    first_gain_grad, second_gain_grad, conv_grad = lax.psum(
        (first_part, second_part, kernel_full), ("dp", "tensor")
    )
    return (
        output,
        input_grad,
        first_gain_grad,
        in_grad,
        conv_grad,
        out_grad,
        second_gain_grad,
        gate_up_grad,
        down_grad,
    )


def solution(mesh):
    in_specs = (
        P(("dp", "tensor"), None),
        P(),
        P(None, "dp", "tensor"),
        P(),
        P("tensor", "dp"),
        P(),
        P(None, "dp", "tensor"),
        P("tensor", "dp"),
        P(("dp", "tensor"), None),
        P(),
    )
    out_specs = (
        P(("dp", "tensor"), None),
        P(("dp", "tensor"), None),
        P(),
        P(None, "dp", "tensor"),
        P(),
        P("tensor", "dp"),
        P(),
        P(None, "dp", "tensor"),
        P("tensor", "dp"),
    )
    return jax.shard_map(shards, mesh=mesh, in_specs=in_specs, out_specs=out_specs, check_vma=False)
```

profile of v0, /device:TPU:0, one launch (start us, length us, event | category | flops | bytes accessed | tf_op | source)
XLA Modules:
  0.0 489.5 jit_solution(4341568830876603250)
XLA Ops:
  7.2 0.7 all-gather.4.cloned.1.call-update
  8.0 0.8 reduce-window.8
  8.8 0.1 convert_reduce_fusion
  8.9 11.7 %all_gather.30 = bf16[256,1024]{1,0:T(8,128)(2,1)S(1)} all-gather(bf16[256,128]{1,0:T(8,128)(2,1)} %param.14), channel_id=1, replica_groups=mesh['dp'=8,'tensor'=4] {'dp'}, dimensions={1}, use_global_device_ids=true | all-gather | bytes 589824 | tf_op jit(solution)/shard_map/all_gather | solution.py:74
  20.6 1.1 fusion.18
  21.8 1.0 fusion.15
  22.8 16.4 %all_gather.28 = bf16[256,1024]{1,0:T(8,128)(2,1)S(1)} all-gather(bf16[64,1024]{1,0:T(8,128)(2,1)S(1)} %fusion.15), channel_id=1, replica_groups=mesh['dp'=8,'tensor'=4] {'tensor'}, dimensions={0}, use_global_device_ids=true | all-gather | bytes 655360 | tf_op jit(solution)/shard_map/all_gather | solution.py:69
  39.2 0.1 fusion.25
  39.3 0.7 fusion.35
  39.9 2.0 convolution_bitcast_fusion.5
  42.0 1.3 collective-permute-start
  43.3 0.9 fusion.34
  44.2 0.9 multiply_convert_fusion.8
  45.1 1.3 fusion.37
  46.4 0.0 all-gather.6.cloned.1.call-start
  46.5 0.7 all-gather.6.cloned.1.call-update
  47.2 0.5 all-gather.8.cloned.1.call-update
  47.8 21.5 %all_gather.34 = bf16[256,1024]{1,0:T(8,128)(2,1)} all-gather(bf16[64,1024]{1,0:T(8,128)(2,1)S(1)} %copy-done.13), channel_id=1, replica_groups=mesh['dp'=8,'tensor'=4] {'tensor'}, dimensions={0}, use_global_device_ids=true | all-gather | bytes 655360 | tf_op jit(solution)/shard_map/all_gather | solution.py:115
  69.3 13.1 %reduce-scatter.9.cloned.1.call-done = f32[64,1024]{1,0:T(8,128)} async-done(((f32[256,1024]{1,0:T(8,128)}), f32[64,1024]{1,0:T(8,128)}) %reduce-scatter.9.cloned.1.call-update) | async-done | bytes 262160 | tf_op jit(solution)/shard_map/reduce_scatter | solution.py:92
  82.4 1.1 multiply_reduce_fusion.5
  83.5 0.1 multiply_convert_fusion.7
  83.6 16.7 %all_gather.31 = bf16[256,1024]{1,0:T(8,128)(2,1)} all-gather(bf16[64,1024]{1,0:T(8,128)(2,1)S(1)} %multiply_convert_fusion.7), channel_id=1, replica_groups=mesh['dp'=8,'tensor'=4] {'tensor'}, dimensions={0}, use_global_device_ids=true | all-gather | bytes 655360 | tf_op jit(solution)/shard_map/all_gather | solution.py:93
  100.3 22.1 %all-gather.6.cloned.1.call-done = bf16[2,1024,1152]{2,1,0:T(8,128)(2,1)} async-done(((bf16[2,128,1152]{2,1,0:T(8,128)(2,1)}), bf16[2,1024,1152]{2,1,0:T(8,128)(2,1)}) %all-gather.6.cloned.1.call-update) | async-done | bytes 4718608 | tf_op jit(solution)/shard_map/all_gather | solution.py:75
  122.4 3.9 convolution_bitcast_fusion.1
  126.2 27.4 %all-gather.8.cloned.1.call-done = bf16[1152,1024]{1,0:T(8,128)(2,1)} async-done(((bf16[1152,128]{1,0:T(8,128)(2,1)}), bf16[1152,1024]{1,0:T(8,128)(2,1)}) %all-gather.8.cloned.1.call-update) | async-done | bytes 2359312 | tf_op jit(solution)/shard_map/all_gather | solution.py:76
  153.6 4.1 fusion.3
  157.7 0.8 copy-done.18
  158.5 0.2 copy-done.20
  158.7 2.4 convolution_bitcast_fusion.4
  161.2 27.2 %reduce-scatter.13.cloned.1.call-done = f32[64,1024]{1,0:T(8,128)} async-done(((f32[256,1024]{1,0:T(8,128)}), f32[64,1024]{1,0:T(8,128)}) %reduce-scatter.13.cloned.1.call-update) | async-done | bytes 262160 | tf_op jit(solution)/shard_map/reduce_scatter | solution.py:129
  188.4 1.2 multiply_reduce_fusion
  189.6 0.5 copy-done.47
  190.1 1.1 fusion.32
  191.3 15.9 %all_gather.35 = bf16[256,1024]{1,0:T(8,128)(2,1)S(1)} all-gather(bf16[64,1024]{1,0:T(8,128)(2,1)S(1)} %fusion.32), channel_id=1, replica_groups=mesh['dp'=8,'tensor'=4] {'tensor'}, dimensions={0}, use_global_device_ids=true | all-gather | bytes 655360 | tf_op jit(solution)/shard_map/all_gather | solution.py:132
  207.2 0.3 fusion.38
  207.6 0.1 fusion.22
  207.7 1.4 collective-permute-start.1
  209.1 1.7 collective-permute-done.1
  210.9 0.8 multiply_reduce_fusion.3
  211.8 1.4 fusion
  213.3 0.0 reduce-scatter.11.cloned.1.call-start
  213.4 3.4 convolution_convert_fusion
  216.8 0.0 reduce-scatter.17.cloned.1.call-start
  216.9 2.3 convolution_bitcast_fusion.2
  219.2 0.0 reduce-scatter.21.cloned.1.call-start
  219.2 1.0 copy-done.3
  220.2 0.2 copy-done.19
  220.4 6.2 %convolution_bitcast_fusion = f32[2,1024,1152]{1,2,0:T(8,128)} fusion(bf16[1,256,1152]{2,1,0:T(8,128)(2,1)} %copy-done.20, bf16[1,256,1152]{2,1,0:T(8,128)(2,1)S(1)} %copy-done.19, bf16[256,1024]{1,0:T(8,128)(2,1)S(1)} %copy-done.3), kind=kOutput, calls=%fused_computation | convolution fusion | flops 1208549376 | bytes 11141120 | tf_op jit(solution)/shard_map/td,ktf->kdf/dot_general | solution.py:123
  226.6 0.0 reduce-scatter.19.cloned.1.call-start
  226.6 0.8 copy-done.16
  227.4 1.3 fusion.39
  228.8 0.0 reduce-scatter.23.cloned.1.call-start
  228.8 3.0 fusion.40
  231.9 0.6 copy-done.42
  232.6 1.5 reduce-scatter.15.cloned.1.call-done
  234.1 1.1 fusion.17
  235.2 39.3 %all-reduce = (f32[1024]{0:T(1024)}, f32[3,1024]{1,0:T(4,128)}, f32[1024]{0:T(1024)}) all-reduce(f32[1024]{0:T(1024)S(1)} %get-tuple-element.32, f32[3,1024]{1,0:T(4,128)S(1)} %maximum_dynamic-update-slice_fusion, f32[1024]{0:T(1024)S(1)} %get-tuple-element.30), channel_id=1, replica_groups=mesh['dp'=8,'tensor'=4] {'dp','tensor'}, use_global_device_ids=true, to_apply=%region_11.12 | all-reduce | flops 5120 | bytes 40960 | tf_op jit(solution)/shard_map/psum | solution.py:177
  274.6 1.9 fusion.14
  276.5 27.7 %reduce-scatter.17.cloned.1.call-done = f32[3,128,256]{1,2,0:T(8,128)} async-done(((f32[3,1024,256]{1,2,0:T(8,128)}), f32[3,128,256]{1,2,0:T(8,128)}) %reduce-scatter.17.cloned.1.call-update) | async-done | bytes 393232 | tf_op jit(solution)/shard_map/reduce_scatter | solution.py:172
  304.2 1.9 copy.25
  306.1 78.5 %reduce-scatter.21.cloned.1.call-done = f32[2,128,1152]{1,2,0:T(8,128)} async-done(((f32[2,1024,1152]{1,2,0:T(8,128)}), f32[2,128,1152]{1,2,0:T(8,128)}) %reduce-scatter.21.cloned.1.call-update) | async-done | bytes 1179664 | tf_op jit(solution)/shard_map/reduce_scatter | solution.py:174
  384.6 2.7 copy.26
  387.3 37.3 %reduce-scatter.19.cloned.1.call-done = f32[256,128]{1,0:T(8,128)} async-done(((f32[256,1024]{1,0:T(8,128)}), f32[256,128]{1,0:T(8,128)}) %reduce-scatter.19.cloned.1.call-update) | async-done | bytes 131088 | tf_op jit(solution)/shard_map/reduce_scatter | solution.py:173
  424.6 58.3 %reduce-scatter.23.cloned.1.call-done = f32[1152,128]{1,0:T(8,128)} async-done(((f32[1152,1024]{1,0:T(8,128)}), f32[1152,128]{1,0:T(8,128)}) %reduce-scatter.23.cloned.1.call-update) | async-done | bytes 589840 | tf_op jit(solution)/shard_map/reduce_scatter | solution.py:175
  (120 shorter events, 0.7 us)
Async XLA Ops:
  7.2 32.7 %all-gather.4.cloned.1.call-start = ((), (), s32[]{:S(2)}) async-start(), calls=%async_computation.8 | async-start | bytes 1769472 | tf_op jit(solution)/shard_map/all_gather | solution.py:73
  7.9 74.5 %reduce-scatter.9.cloned.1.call-start = ((), (), s32[]{:S(2)}) async-start(), calls=%async_computation.9 | async-start | bytes 1310720 | tf_op jit(solution)/shard_map/reduce_scatter | solution.py:92
  20.6 24.5 %copy-start.4 = (bf16[256,1024]{1,0:T(8,128)(2,1)}, bf16[256,1024]{1,0:T(8,128)(2,1)S(1)}, u32[]{:S(2)}) copy-start(bf16[256,1024]{1,0:T(8,128)(2,1)S(1)} %all_gather.30) | copy-start | bytes 1572868
  21.8 17.5 %copy-start.40 = (f32[64]{0:T(128)}, f32[64]{0:T(128)S(1)}, u32[]{:S(2)}) copy-start(f32[64]{0:T(128)S(1)} %add_rsqrt_fusion.1) | copy-start | bytes 772
  39.2 2.8 copy-start.6
  39.9 4.3 copy-start.33
  39.9 4.3 copy-start.35
  42.0 2.2 collective-permute-start
  44.2 0.9 copy-start.27
  44.2 0.9 copy-start.29
  44.2 0.9 copy-start.31
  45.1 2.1 copy-start.15
  45.1 2.7 copy-start.13
  46.4 36.0 %copy-start.8 = (bf16[64,1024]{1,0:T(8,128)(2,1)S(1)}, bf16[64,1024]{1,0:T(8,128)(2,1)}, u32[]{:S(2)}) copy-start(bf16[64,1024]{1,0:T(8,128)(2,1)} %param.10) | copy-start | bytes 393220
  46.4 37.1 %copy-start.25 = (f32[1024]{0:T(1024)S(1)}, f32[1024]{0:T(1024)}, u32[]{:S(2)}) copy-start(f32[1024]{0:T(1024)} %param.15) | copy-start | bytes 12292
  46.4 75.9 %all-gather.6.cloned.1.call-start = ((), (), s32[]{:S(2)}) async-start(), calls=%async_computation.10 | async-start | bytes 5308416 | tf_op jit(solution)/shard_map/all_gather | solution.py:75
  47.2 106.4 %all-gather.8.cloned.1.call-start = ((), (), s32[]{:S(2)}) async-start(), calls=%async_computation.11 | async-start | bytes 2654208 | tf_op jit(solution)/shard_map/all_gather | solution.py:76
  47.8 140.6 %reduce-scatter.13.cloned.1.call-start = ((), (), s32[]{:S(2)}) async-start(), calls=%async_computation.13 | async-start | bytes 1310720 | tf_op jit(solution)/shard_map/reduce_scatter | solution.py:129
  83.5 16.8 %copy-start.1 = (f32[64,1024]{1,0:T(8,128)}, f32[64,1024]{1,0:T(8,128)S(1)}, u32[]{:S(2)}) copy-start(f32[64,1024]{1,0:T(8,128)S(1)} %get-tuple-element.40) | copy-start | bytes 786436
  83.5 16.8 %copy-start.37 = (f32[64]{0:T(128)}, f32[64]{0:T(128)S(1)}, u32[]{:S(2)}) copy-start(f32[64]{0:T(128)S(1)} %add_rsqrt_fusion) | copy-start | bytes 772
  153.6 5.1 %copy-start = (bf16[2,1024,1152]{2,1,0:T(8,128)(2,1)S(1)}, bf16[2,1024,1152]{2,1,0:T(8,128)(2,1)}, u32[]{:S(2)}) copy-start(bf16[2,1024,1152]{2,1,0:T(8,128)(2,1)} %all-gather.6.cloned.1.call-done) | copy-start | bytes 14155780
  157.7 0.8 copy-start.18
  157.7 1.0 copy-start.20
  158.7 29.7 %copy-start.2 = (f32[64,1024]{1,0:T(8,128)S(1)}, f32[64,1024]{1,0:T(8,128)}, u32[]{:S(2)}) copy-start(f32[64,1024]{1,0:T(8,128)} %copy-done.1) | copy-start | bytes 786436
  158.7 29.7 %copy-start.38 = (f32[64]{0:T(128)S(1)}, f32[64]{0:T(128)}, u32[]{:S(2)}) copy-start(f32[64]{0:T(128)} %copy-done.37) | copy-start | bytes 772
  161.1 29.0 %copy-start.14 = (bf16[64,1024]{1,0:T(8,128)(2,1)S(1)}, bf16[64,1024]{1,0:T(8,128)(2,1)}, u32[]{:S(2)}) copy-start(bf16[64,1024]{1,0:T(8,128)(2,1)} %param.18) | copy-start | bytes 393220
  161.1 46.1 %copy-start.5 = (bf16[256,1024]{1,0:T(8,128)(2,1)S(1)}, bf16[256,1024]{1,0:T(8,128)(2,1)}, u32[]{:S(2)}) copy-start(bf16[256,1024]{1,0:T(8,128)(2,1)} %copy-done.4) | copy-start | bytes 1572868
  161.1 46.4 %copy-start.17 = (f32[256,256]{1,0:T(8,128)S(1)}, f32[256,256]{1,0:T(8,128)}, u32[]{:S(2)}) copy-start(f32[256,256]{1,0:T(8,128)} %get-tuple-element.42) | copy-start | bytes 786436
  161.1 73.0 %reduce-scatter.15.cloned.1.call-start = ((), (), s32[]{:S(2)}) async-start(), calls=%async_computation.14 | async-start | bytes 655360 | tf_op jit(solution)/shard_map/reduce_scatter | solution.py:166
  189.6 0.5 copy-start.47
  191.2 19.6 %copy-start.28 = (f32[1,256]{1,0:T(1,128)S(1)}, f32[1,256]{1,0:T(1,128)}, u32[]{:S(2)}) copy-start(f32[1,256]{1,0:T(1,128)} %copy-done.27) | copy-start | bytes 3076
  191.2 19.6 %copy-start.30 = (f32[1,256]{1,0:T(1,128)S(1)}, f32[1,256]{1,0:T(1,128)}, u32[]{:S(2)}) copy-start(f32[1,256]{1,0:T(1,128)} %copy-done.29) | copy-start | bytes 3076
  191.2 19.6 %copy-start.32 = (f32[1,256]{1,0:T(1,128)S(1)}, f32[1,256]{1,0:T(1,128)}, u32[]{:S(2)}) copy-start(f32[1,256]{1,0:T(1,128)} %copy-done.31) | copy-start | bytes 3076
  191.2 19.6 %copy-start.34 = (f32[256]{0:T(256)S(1)}, f32[256]{0:T(256)}, u32[]{:S(2)}) copy-start(f32[256]{0:T(256)} %copy-done.33) | copy-start | bytes 3076
  191.2 19.6 %copy-start.36 = (f32[256]{0:T(256)S(1)}, f32[256]{0:T(256)}, u32[]{:S(2)}) copy-start(f32[256]{0:T(256)} %copy-done.35) | copy-start | bytes 3076
  191.3 19.6 %copy-start.45 = (f32[256]{0:T(256)S(1)}, f32[256]{0:T(256)}, u32[]{:S(2)}) copy-start(f32[256]{0:T(256)} %get-tuple-element.57) | copy-start | bytes 3076
  191.3 19.6 %copy-start.46 = (f32[256]{0:T(256)S(1)}, f32[256]{0:T(256)}, u32[]{:S(2)}) copy-start(f32[256]{0:T(256)} %get-tuple-element.62) | copy-start | bytes 3076
  207.6 4.2 copy-start.23
  207.7 4.2 copy-start.11
  207.7 3.2 collective-permute-start.1
  211.8 1.5 copy-start.21
  211.8 1.5 copy-start.12
  213.3 61.3 %reduce-scatter.11.cloned.1.call-start = ((), (), s32[]{:S(2)}) async-start(), calls=%async_computation.12 | async-start | bytes 655360 | tf_op jit(solution)/shard_map/reduce_scatter | solution.py:105
  213.3 3.5 copy-start.7
  213.3 3.5 copy-start.22
  213.4 3.5 copy-start.24
  216.8 87.4 %reduce-scatter.17.cloned.1.call-start = ((), (), s32[]{:S(2)}) async-start(), calls=%async_computation.15 | async-start | bytes 3538944 | tf_op jit(solution)/shard_map/reduce_scatter | solution.py:172
  219.1 1.0 copy-start.3
  219.1 1.2 copy-start.19
  219.2 165.5 %reduce-scatter.21.cloned.1.call-start = ((), (), s32[]{:S(2)}) async-start(), calls=%async_computation.17 | async-start | bytes 10616832 | tf_op jit(solution)/shard_map/reduce_scatter | solution.py:174
  226.5 0.9 copy-start.16
  226.6 2.3 copy-start.10
  226.6 198.1 %reduce-scatter.19.cloned.1.call-start = ((), (), s32[]{:S(2)}) async-start(), calls=%async_computation.16 | async-start | bytes 1179648 | tf_op jit(solution)/shard_map/reduce_scatter | solution.py:173
  228.8 254.2 %reduce-scatter.23.cloned.1.call-start = ((), (), s32[]{:S(2)}) async-start(), calls=%async_computation.18 | async-start | bytes 5308416 | tf_op jit(solution)/shard_map/reduce_scatter | solution.py:175
  231.9 0.7 copy-start.42
  231.9 0.7 copy-start.43
  231.9 0.7 copy-start.44
  231.9 2.2 copy-start.26
  231.9 2.2 copy-start.41
  231.9 42.7 %copy-start.9 = (f32[64,1024]{1,0:T(8,128)S(1)}, f32[64,1024]{1,0:T(8,128)}, u32[]{:S(2)}) copy-start(f32[64,1024]{1,0:T(8,128)} %reduce-scatter.13.cloned.1.call-done) | copy-start | bytes 786436
  231.9 42.7 %copy-start.39 = (f32[64]{0:T(128)S(1)}, f32[64]{0:T(128)}, u32[]{:S(2)}) copy-start(f32[64]{0:T(128)} %copy-done.37) | copy-start | bytes 772
  231.9 42.7 %copy-start.48 = (f32[64]{0:T(128)S(1)}, f32[64]{0:T(128)}, u32[]{:S(2)}) copy-start(f32[64]{0:T(128)} %copy-done.47) | copy-start | bytes 772
Sparse Core Ops, SparseCore 0:
  9.9 28.3 all-gather.3
  46.6 35.7 reduce-scatter.8
  84.4 37.8 all-gather.5
  124.2 29.3 all-gather.7
  161.2 27.1 reduce-scatter.12
  213.4 20.6 reduce-scatter.14
  236.4 19.9 reduce-scatter.10
  259.8 44.4 reduce-scatter.16
  308.1 76.4 reduce-scatter.20
  388.6 36.0 reduce-scatter.18
  429.0 53.8 reduce-scatter.22
where the time goes:
time: 490 us; the launch traced here: 489 us
  waiting for transfers between devices  297 us (61%)
  blocking collectives  121 us (25%)
  matrix products  31.5 us (6%)
  between operations  14.5 us (3%)
  other arithmetic  11.5 us (2%)
  local copies, waits for them, and re-layouts  10.4 us (2%)
    reduce_scatter x1, waiting for transfers between devices, shards(): lax.psum_scatter(gate_up_part, 'dp', scatter_dimension=1, tiled=True)  78.5 us
    reduce_scatter x1, waiting for transfers between devices, shards(): lax.psum_scatter(down_part, 'dp', scatter_dimension=1, tiled=True)  58.3 us
    psum x1, blocking collectives, shards(): lax.psum((first_part, second_part, kernel_full), ('dp', 'tensor'))  39.3 us
    reduce_scatter x1, waiting for transfers between devices, shards(): lax.psum_scatter(out_part, 'dp', scatter_dimension=1, tiled=True)  37.3 us
    reduce_scatter x1, waiting for transfers between devices, shards(): lax.psum_scatter(in_part, 'dp', scatter_dimension=1, tiled=True)  27.7 us
    all_gather x1, waiting for transfers between devices, shards(): lax.all_gather(down_weight, 'dp', axis=1, tiled=True)  27.4 us
    reduce_scatter x1, waiting for transfers between devices, shards(): lax.psum_scatter(hidden_back, 'tensor', scatter_dimension=0, tiled=True)  27.2 us
    all_gather x1, waiting for transfers between devices, shards(): lax.all_gather(gate_up_weight, 'dp', axis=1, tiled=True)  22.1 us
  transfers between devices with their start and end apart: 13, of which 10 were waited for; matrix products, arithmetic and copies ran while one was open for 7% of the time, Pallas kernels for 0%

commit v1 on v0

--- a/solution.py
+++ b/solution.py
@@ -4,6 +4,27 @@
 from jax.sharding import PartitionSpec as P
 
 EPS = 1e-05
+
+
+def ring_gather(value, axis, dim):
+    count, index, width = (lax.axis_size(axis), lax.axis_index(axis), value.shape[dim])
+    right = [(i, (i + 1) % count) for i in range(count)]
+    downward = [(i, (i - 1) % count) for i in range(count)]
+    out = jnp.zeros((*value.shape[:dim], count * width, *value.shape[dim + 1 :]), value.dtype)
+    out = lax.dynamic_update_slice_in_dim(out, value, index * width, axis=dim)
+    from_left = from_right = value
+    half = count // 2
+    for step in range(1, half + 1):
+        from_left = lax.ppermute(from_left, axis, right)
+        out = lax.dynamic_update_slice_in_dim(
+            out, from_left, (index - step) % count * width, axis=dim
+        )
+        if step < count - half:
+            from_right = lax.ppermute(from_right, axis, downward)
+            out = lax.dynamic_update_slice_in_dim(
+                out, from_right, (index + step) % count * width, axis=dim
+            )
+    return out
 
 
 def passed_along(block, axis, distance):
@@ -73,7 +94,7 @@
         lax.all_gather(entry_projection_weight, "dp", axis=1, tiled=True),
         lax.all_gather(out_weight, "dp", axis=1, tiled=True),
         lax.all_gather(gate_up_weight, "dp", axis=1, tiled=True),
-        lax.all_gather(down_weight, "dp", axis=1, tiled=True),
+        ring_gather(down_weight, "dp", 1),
     )
     projected = jnp.einsum("td,kdc->ktc", normed, in_full, preferred_element_type=jnp.float32)
     input_gate_value = projected[0]

time: 490 us -> 490 us (level)
  waiting for transfers between devices: 297 us -> 276 us
  local copies, waits for them, and re-layouts: 10.4 us -> 22.3 us
  starting transfers between devices: 3.16 us -> 13.1 us
    reduce_scatter x1, waiting for transfers between devices: 27.2 us -> 5.17 us  [shards(): lax.psum_scatter(hidden_back, 'tensor', scatter_dimension=0, tiled=True)]
    ppermute x0 -> x7, waiting for transfers between devices: none -> 12.5 us  [the longest x4 12.5 us: ring_gather(): from_left = lax.ppermute(from_left, axis, right)]
    dynamic_update_slice x0 -> x8, local copies, waits for them, and re-layouts: none -> 9.98 us  [the longest x4 5.02 us: ring_gather(): lax.dynamic_update_slice_in_dim(out, from_left, (index - step) % count *...]
    ppermute x0 -> x7, starting transfers between devices: none -> 9.73 us  [the longest x3 7.66 us: ring_gather(): from_right = lax.ppermute(from_right, axis, downward)]
    reduce_scatter x1, waiting for transfers between devices: 27.7 us -> 20.1 us  [shards(): lax.psum_scatter(in_part, 'dp', scatter_dimension=1, tiled=True)]
  transfers between devices with their start and end apart: 13 -> 20, of which waited for: 10 -> 11; matrix products, arithmetic and copies ran while one was open for 7% -> 10% of each run, Pallas kernels for 0% -> 0%
where the time goes in v1:
time: 490 us
  waiting for transfers between devices  276 us (56%)
  blocking collectives  121 us (25%)
  matrix products  31.5 us (6%)
  local copies, waits for them, and re-layouts  22.3 us (5%)
  between operations  14.5 us (3%)
  starting transfers between devices  13.1 us (3%)
  other arithmetic  11.6 us (2%)
    reduce_scatter x1, waiting for transfers between devices, shards(): lax.psum_scatter(gate_up_part, 'dp', scatter_dimension=1, tiled=True)  78.5 us
    reduce_scatter x1, waiting for transfers between devices, shards(): lax.psum_scatter(down_part, 'dp', scatter_dimension=1, tiled=True)  58.3 us
    psum x1, blocking collectives, shards(): lax.psum((first_part, second_part, kernel_full), ('dp', 'tensor'))  38.4 us
    reduce_scatter x1, waiting for transfers between devices, shards(): lax.psum_scatter(out_part, 'dp', scatter_dimension=1, tiled=True)  37.4 us
    all_gather x1, waiting for transfers between devices, shards(): lax.all_gather(down_weight, 'dp', axis=1, tiled=True)  27.4 us
    all_gather x1, blocking collectives, shards(): grad_rows = lax.all_gather(cotangent, 'tensor', axis=0, tiled=True)  21.6 us
    all_gather x1, waiting for transfers between devices, shards(): lax.all_gather(gate_up_weight, 'dp', axis=1, tiled=True)  21.4 us
    reduce_scatter x1, waiting for transfers between devices, shards(): lax.psum_scatter(in_part, 'dp', scatter_dimension=1, tiled=True)  20.1 us
  transfers between devices with their start and end apart: 20, of which 11 were waited for; matrix products, arithmetic and copies ran while one was open for 10% of the time, Pallas kernels for 0%

profile of v1, /device:TPU:0, one launch (start us, length us, event | category | flops | bytes accessed | tf_op | source)
XLA Modules:
  0.0 489.6 jit_solution(7393284943011213073)
XLA Ops:
  7.2 0.7 all-gather.4.cloned.1.call-update
  8.0 0.8 reduce-window.8
  8.9 11.7 %all_gather.29 = bf16[256,1024]{1,0:T(8,128)(2,1)S(1)} all-gather(bf16[256,128]{1,0:T(8,128)(2,1)} %param.14), channel_id=1, replica_groups=mesh['dp'=8,'tensor'=4] {'dp'}, dimensions={1}, use_global_device_ids=true | all-gather | bytes 589824 | tf_op jit(solution)/shard_map/all_gather | solution.py:95
  20.6 1.1 fusion.18
  21.8 1.0 fusion.15
  22.8 16.4 %all_gather.27 = bf16[256,1024]{1,0:T(8,128)(2,1)S(1)} all-gather(bf16[64,1024]{1,0:T(8,128)(2,1)S(1)} %fusion.15), channel_id=1, replica_groups=mesh['dp'=8,'tensor'=4] {'tensor'}, dimensions={0}, use_global_device_ids=true | all-gather | bytes 655360 | tf_op jit(solution)/shard_map/all_gather | solution.py:90
  39.2 0.7 fusion.35
  39.9 2.0 convolution_bitcast_fusion.5
  42.0 1.3 collective-permute-start
  43.3 0.9 fusion.34
  44.2 0.9 multiply_convert_fusion.8
  45.1 1.3 fusion.37
  46.5 0.7 all-gather.6.cloned.1.call-update
  47.8 21.6 %all_gather.32 = bf16[256,1024]{1,0:T(8,128)(2,1)} all-gather(bf16[64,1024]{1,0:T(8,128)(2,1)S(1)} %copy-done.14), channel_id=1, replica_groups=mesh['dp'=8,'tensor'=4] {'tensor'}, dimensions={0}, use_global_device_ids=true | all-gather | bytes 655360 | tf_op jit(solution)/shard_map/all_gather | solution.py:136
  69.4 13.0 %reduce-scatter.9.cloned.1.call-done = f32[64,1024]{1,0:T(8,128)} async-done(((f32[256,1024]{1,0:T(8,128)}), f32[64,1024]{1,0:T(8,128)}) %reduce-scatter.9.cloned.1.call-update) | async-done | bytes 262160 | tf_op jit(solution)/shard_map/reduce_scatter | solution.py:113
  82.4 1.1 multiply_reduce_fusion.5
  83.5 0.7 copy-done.1
  84.3 16.7 %all_gather.30 = bf16[256,1024]{1,0:T(8,128)(2,1)} all-gather(bf16[64,1024]{1,0:T(8,128)(2,1)S(1)} %multiply_convert_fusion.7), channel_id=1, replica_groups=mesh['dp'=8,'tensor'=4] {'tensor'}, dimensions={0}, use_global_device_ids=true | all-gather | bytes 655360 | tf_op jit(solution)/shard_map/all_gather | solution.py:114
  101.0 21.4 %all-gather.6.cloned.1.call-done = bf16[2,1024,1152]{2,1,0:T(8,128)(2,1)} async-done(((bf16[2,128,1152]{2,1,0:T(8,128)(2,1)}), bf16[2,1024,1152]{2,1,0:T(8,128)(2,1)}) %all-gather.6.cloned.1.call-update) | async-done | bytes 4718608 | tf_op jit(solution)/shard_map/all_gather | solution.py:96
  122.4 3.9 convolution_bitcast_fusion.1
  126.3 27.4 %all-gather.8.cloned.1.call-done = bf16[1152,1024]{1,0:T(8,128)(2,1)} async-done(((bf16[1152,128]{1,0:T(8,128)(2,1)}), bf16[1152,1024]{1,0:T(8,128)(2,1)}) %all-gather.8.cloned.1.call-update) | async-done | bytes 2359312 | tf_op jit(solution)/shard_map/all_gather | solution.py:134
  153.6 4.1 fusion.3
  157.7 0.8 copy-done.19
  158.7 2.4 convolution_bitcast_fusion.4
  161.6 2.4 collective-permute-start.2
  163.9 1.7 broadcast_in_dim.4
  165.7 0.8 constant_dynamic-update-slice_fusion.7
  166.5 4.2 collective-permute-done.1
  170.7 2.6 collective-permute-start.4
  173.3 0.8 constant_dynamic-update-slice_fusion.6
  174.1 0.8 constant_dynamic-update-slice_fusion.5
  174.9 5.8 %collective-permute-done.3 = bf16[1152,128]{1,0:T(8,128)(2,1)} collective-permute-done((bf16[1152,128]{1,0:T(8,128)(2,1)S(1)}, bf16[1152,128]{1,0:T(8,128)(2,1)}, u32[]{:S(2)}, u32[]{:S(2)}) %collective-permute-start.3) | collective-permute-done | bytes 294944 | tf_op jit(solution)/shard_map/ppermute | solution.py:18
  180.6 2.6 collective-permute-start.6
  183.3 5.2 %reduce-scatter.13.cloned.1.call-done = f32[64,1024]{1,0:T(8,128)} async-done(((f32[256,1024]{1,0:T(8,128)}), f32[64,1024]{1,0:T(8,128)}) %reduce-scatter.13.cloned.1.call-update) | async-done | bytes 262160 | tf_op jit(solution)/shard_map/reduce_scatter | solution.py:150
  188.5 1.2 multiply_reduce_fusion
  189.8 1.1 fusion.32
  190.9 16.1 %all_gather.34 = bf16[256,1024]{1,0:T(8,128)(2,1)S(1)} all-gather(bf16[64,1024]{1,0:T(8,128)(2,1)S(1)} %fusion.32), channel_id=1, replica_groups=mesh['dp'=8,'tensor'=4] {'tensor'}, dimensions={0}, use_global_device_ids=true | all-gather | bytes 655360 | tf_op jit(solution)/shard_map/all_gather | solution.py:153
  207.4 1.4 collective-permute-start.8
  208.8 1.7 constant_dynamic-update-slice_fusion.4
  210.6 0.8 multiply_reduce_fusion.3
  211.6 1.4 fusion
  213.0 1.7 constant_dynamic-update-slice_fusion.3
  214.8 1.7 collective-permute-start.7
  216.5 1.7 constant_dynamic-update-slice_fusion.2
  218.2 1.7 constant_dynamic-update-slice_fusion.1
  219.9 2.5 collective-permute-done.7
  222.5 0.8 constant_dynamic-update-slice_fusion
  223.3 3.4 convolution_convert_fusion
  226.8 2.3 convolution_bitcast_fusion.2
  229.1 1.0 copy-done.3
  230.3 6.1 %convolution_bitcast_fusion = f32[2,1024,1152]{1,2,0:T(8,128)} fusion(bf16[1,256,1152]{2,1,0:T(8,128)(2,1)} %copy-done.21, bf16[1,256,1152]{2,1,0:T(8,128)(2,1)S(1)} %copy-done.20, bf16[256,1024]{1,0:T(8,128)(2,1)S(1)} %copy-done.3), kind=kOutput, calls=%fused_computation | convolution fusion | flops 1208549376 | bytes 11141120 | tf_op jit(solution)/shard_map/td,ktf->kdf/dot_general | solution.py:144
  236.5 0.8 copy-done.17
  237.3 1.3 fusion.39
  238.9 3.0 fusion.40
  242.0 0.6 copy-done.43
  242.7 1.1 fusion.17
  243.8 38.4 %all-reduce = (f32[1024]{0:T(1024)}, f32[3,1024]{1,0:T(4,128)}, f32[1024]{0:T(1024)}) all-reduce(f32[1024]{0:T(1024)S(1)} %get-tuple-element.32, f32[3,1024]{1,0:T(4,128)S(1)} %maximum_dynamic-update-slice_fusion, f32[1024]{0:T(1024)S(1)} %get-tuple-element.30), channel_id=1, replica_groups=mesh['dp'=8,'tensor'=4] {'dp','tensor'}, use_global_device_ids=true, to_apply=%region_11.12 | all-reduce | flops 5120 | bytes 40960 | tf_op jit(solution)/shard_map/psum | solution.py:198
  282.3 1.9 fusion.14
  284.2 20.1 %reduce-scatter.17.cloned.1.call-done = f32[3,128,256]{1,2,0:T(8,128)} async-done(((f32[3,1024,256]{1,2,0:T(8,128)}), f32[3,128,256]{1,2,0:T(8,128)}) %reduce-scatter.17.cloned.1.call-update) | async-done | bytes 393232 | tf_op jit(solution)/shard_map/reduce_scatter | solution.py:193
  304.3 1.9 copy.25
  306.2 78.5 %reduce-scatter.21.cloned.1.call-done = f32[2,128,1152]{1,2,0:T(8,128)} async-done(((f32[2,1024,1152]{1,2,0:T(8,128)}), f32[2,128,1152]{1,2,0:T(8,128)}) %reduce-scatter.21.cloned.1.call-update) | async-done | bytes 1179664 | tf_op jit(solution)/shard_map/reduce_scatter | solution.py:195
  384.7 2.7 copy.26
  387.4 37.4 %reduce-scatter.19.cloned.1.call-done = f32[256,128]{1,0:T(8,128)} async-done(((f32[256,1024]{1,0:T(8,128)}), f32[256,128]{1,0:T(8,128)}) %reduce-scatter.19.cloned.1.call-update) | async-done | bytes 131088 | tf_op jit(solution)/shard_map/reduce_scatter | solution.py:194
  424.7 58.3 %reduce-scatter.23.cloned.1.call-done = f32[1152,128]{1,0:T(8,128)} async-done(((f32[1152,1024]{1,0:T(8,128)}), f32[1152,128]{1,0:T(8,128)}) %reduce-scatter.23.cloned.1.call-update) | async-done | bytes 589840 | tf_op jit(solution)/shard_map/reduce_scatter | solution.py:196
  (145 shorter events, 3.1 us)
Async XLA Ops:
  7.2 32.7 %all-gather.4.cloned.1.call-start = ((), (), s32[]{:S(2)}) async-start(), calls=%async_computation.8 | async-start | bytes 1769472 | tf_op jit(solution)/shard_map/all_gather | solution.py:94
  7.9 74.5 %reduce-scatter.9.cloned.1.call-start = ((), (), s32[]{:S(2)}) async-start(), calls=%async_computation.9 | async-start | bytes 1310720 | tf_op jit(solution)/shard_map/reduce_scatter | solution.py:113
  20.6 24.5 %copy-start.4 = (bf16[256,1024]{1,0:T(8,128)(2,1)}, bf16[256,1024]{1,0:T(8,128)(2,1)S(1)}, u32[]{:S(2)}) copy-start(bf16[256,1024]{1,0:T(8,128)(2,1)S(1)} %all_gather.29) | copy-start | bytes 1572868
  21.8 22.4 %copy-start.41 = (f32[64]{0:T(128)}, f32[64]{0:T(128)S(1)}, u32[]{:S(2)}) copy-start(f32[64]{0:T(128)S(1)} %add_rsqrt_fusion.1) | copy-start | bytes 772
  39.2 5.9 %copy-start.6 = (bf16[256,1024]{1,0:T(8,128)(2,1)}, bf16[256,1024]{1,0:T(8,128)(2,1)S(1)}, u32[]{:S(2)}) copy-start(bf16[256,1024]{1,0:T(8,128)(2,1)S(1)} %all_gather.27) | copy-start | bytes 1572868
  39.9 5.2 %copy-start.34 = (f32[256]{0:T(256)}, f32[256]{0:T(256)S(1)}, u32[]{:S(2)}) copy-start(f32[256]{0:T(256)S(1)} %get-tuple-element.58) | copy-start | bytes 3076
  39.9 5.2 %copy-start.36 = (f32[256]{0:T(256)}, f32[256]{0:T(256)S(1)}, u32[]{:S(2)}) copy-start(f32[256]{0:T(256)S(1)} %get-tuple-element.61) | copy-start | bytes 3076
  42.0 2.2 collective-permute-start
  44.1 3.0 copy-start.28
  44.1 3.0 copy-start.30
  44.2 3.0 copy-start.32
  44.2 3.6 copy-start.14
  45.1 38.4 %copy-start.16 = (bf16[256,256]{1,0:T(8,128)(2,1)}, bf16[256,256]{1,0:T(8,128)(2,1)S(1)}, u32[]{:S(2)}) copy-start(bf16[256,256]{1,0:T(8,128)(2,1)S(1)} %get-tuple-element.41) | copy-start | bytes 393220
  45.1 37.3 %copy-start.8 = (bf16[64,1024]{1,0:T(8,128)(2,1)S(1)}, bf16[64,1024]{1,0:T(8,128)(2,1)}, u32[]{:S(2)}) copy-start(bf16[64,1024]{1,0:T(8,128)(2,1)} %param.10) | copy-start | bytes 393220
  45.1 39.1 %copy-start.26 = (f32[1024]{0:T(1024)S(1)}, f32[1024]{0:T(1024)}, u32[]{:S(2)}) copy-start(f32[1024]{0:T(1024)} %param.15) | copy-start | bytes 12292
  46.4 75.9 %all-gather.6.cloned.1.call-start = ((), (), s32[]{:S(2)}) async-start(), calls=%async_computation.10 | async-start | bytes 5308416 | tf_op jit(solution)/shard_map/all_gather | solution.py:96
  47.2 106.4 %all-gather.8.cloned.1.call-start = ((), (), s32[]{:S(2)}) async-start(), calls=%async_computation.12 | async-start | bytes 2654208 | tf_op jit(solution)/shard_map/all_gather | solution.py:134
  47.8 140.7 %reduce-scatter.13.cloned.1.call-start = ((), (), s32[]{:S(2)}) async-start(), calls=%async_computation.13 | async-start | bytes 1310720 | tf_op jit(solution)/shard_map/reduce_scatter | solution.py:150
  83.5 0.8 copy-start.38
  153.6 5.1 %copy-start = (bf16[2,1024,1152]{2,1,0:T(8,128)(2,1)S(1)}, bf16[2,1024,1152]{2,1,0:T(8,128)(2,1)}, u32[]{:S(2)}) copy-start(bf16[2,1024,1152]{2,1,0:T(8,128)(2,1)} %all-gather.6.cloned.1.call-done) | copy-start | bytes 14155780
  157.7 0.8 copy-start.19
  157.7 1.0 copy-start.21
  158.7 2.5 copy-start.13
  161.2 27.3 %copy-start.2 = (f32[64,1024]{1,0:T(8,128)S(1)}, f32[64,1024]{1,0:T(8,128)}, u32[]{:S(2)}) copy-start(f32[64,1024]{1,0:T(8,128)} %copy-done.1) | copy-start | bytes 786436
  161.2 27.3 %copy-start.39 = (f32[64]{0:T(128)S(1)}, f32[64]{0:T(128)}, u32[]{:S(2)}) copy-start(f32[64]{0:T(128)} %copy-done.38) | copy-start | bytes 772
  161.2 81.5 %reduce-scatter.15.cloned.1.call-start = ((), (), s32[]{:S(2)}) async-start(), calls=%async_computation.14 | async-start | bytes 655360 | tf_op jit(solution)/shard_map/reduce_scatter | solution.py:187
  161.2 9.4 %collective-permute-start.1 = (bf16[1152,128]{1,0:T(8,128)(2,1)S(1)}, bf16[1152,128]{1,0:T(8,128)(2,1)S(1)}, u32[]{:S(2)}, u32[]{:S(2)}) collective-permute-start(bf16[1152,128]{1,0:T(8,128)(2,1)S(1)} %copy-done.13), channel_id=1, source_target_pairs={{0,4},{4,8},{8,12},{12,16},{16,20},{20,24},{24,28},{28,0},{1,5},{5... | collective-permute-start | bytes 884744 | tf_op jit(solution)/shard_map/ppermute | solution.py:18
  161.6 9.1 %collective-permute-start.2 = (bf16[1152,128]{1,0:T(8,128)(2,1)S(1)}, bf16[1152,128]{1,0:T(8,128)(2,1)S(1)}, u32[]{:S(2)}, u32[]{:S(2)}) collective-permute-start(bf16[1152,128]{1,0:T(8,128)(2,1)S(1)} %copy-done.13), channel_id=1, source_target_pairs={{0,28},{4,0},{8,4},{12,8},{16,12},{20,16},{24,20},{28,24},{1,29},{... | collective-permute-start | bytes 884744 | tf_op jit(solution)/shard_map/ppermute | solution.py:23
  163.9 25.7 %copy-start.15 = (bf16[64,1024]{1,0:T(8,128)(2,1)S(1)}, bf16[64,1024]{1,0:T(8,128)(2,1)}, u32[]{:S(2)}) copy-start(bf16[64,1024]{1,0:T(8,128)(2,1)} %param.18) | copy-start | bytes 393220
  165.7 41.2 %copy-start.5 = (bf16[256,1024]{1,0:T(8,128)(2,1)S(1)}, bf16[256,1024]{1,0:T(8,128)(2,1)}, u32[]{:S(2)}) copy-start(bf16[256,1024]{1,0:T(8,128)(2,1)} %copy-done.4) | copy-start | bytes 1572868
  166.5 40.8 %copy-start.18 = (f32[256,256]{1,0:T(8,128)S(1)}, f32[256,256]{1,0:T(8,128)}, u32[]{:S(2)}) copy-start(f32[256,256]{1,0:T(8,128)} %get-tuple-element.42) | copy-start | bytes 786436
  170.7 10.0 %collective-permute-start.3 = (bf16[1152,128]{1,0:T(8,128)(2,1)S(1)}, bf16[1152,128]{1,0:T(8,128)(2,1)}, u32[]{:S(2)}, u32[]{:S(2)}) collective-permute-start(bf16[1152,128]{1,0:T(8,128)(2,1)S(1)} %collective-permute-done.1), channel_id=1, source_target_pairs={{0,4},{4,8},{8,12},{12,16},{16,20},{20,24},{24,28},{28,0},{1,5},{5... | collective-permute-start | bytes 884744 | tf_op jit(solution)/shard_map/ppermute | solution.py:18
  170.7 10.0 %collective-permute-start.4 = (bf16[1152,128]{1,0:T(8,128)(2,1)S(1)}, bf16[1152,128]{1,0:T(8,128)(2,1)}, u32[]{:S(2)}, u32[]{:S(2)}) collective-permute-start(bf16[1152,128]{1,0:T(8,128)(2,1)S(1)} %collective-permute-done.2), channel_id=1, source_target_pairs={{0,28},{4,0},{8,4},{12,8},{16,12},{20,16},{24,20},{28,24},{1,29},{... | collective-permute-start | bytes 884744 | tf_op jit(solution)/shard_map/ppermute | solution.py:23
  180.6 34.1 %collective-permute-start.5 = (bf16[1152,128]{1,0:T(8,128)(2,1)}, bf16[1152,128]{1,0:T(8,128)(2,1)}, u32[]{:S(2)}, u32[]{:S(2)}) collective-permute-start(bf16[1152,128]{1,0:T(8,128)(2,1)} %collective-permute-done.3), channel_id=1, source_target_pairs={{0,4},{4,8},{8,12},{12,16},{16,20},{20,24},{24,28},{28,0},{1,5},{5... | collective-permute-start | bytes 884744 | tf_op jit(solution)/shard_map/ppermute | solution.py:18
  180.6 37.6 %collective-permute-start.6 = (bf16[1152,128]{1,0:T(8,128)(2,1)}, bf16[1152,128]{1,0:T(8,128)(2,1)}, u32[]{:S(2)}, u32[]{:S(2)}) collective-permute-start(bf16[1152,128]{1,0:T(8,128)(2,1)} %collective-permute-done.4), channel_id=1, source_target_pairs={{0,28},{4,0},{8,4},{12,8},{16,12},{20,16},{24,20},{28,24},{1,29},{... | collective-permute-start | bytes 884744 | tf_op jit(solution)/shard_map/ppermute | solution.py:23
  189.7 20.9 %copy-start.48 = (f32[64]{0:T(128)}, f32[64]{0:T(128)S(1)}, u32[]{:S(2)}) copy-start(f32[64]{0:T(128)S(1)} %broadcast_multiply_fusion.1) | copy-start | bytes 772
  189.7 20.9 %copy-start.29 = (f32[1,256]{1,0:T(1,128)S(1)}, f32[1,256]{1,0:T(1,128)}, u32[]{:S(2)}) copy-start(f32[1,256]{1,0:T(1,128)} %copy-done.28) | copy-start | bytes 3076
  189.7 20.9 %copy-start.31 = (f32[1,256]{1,0:T(1,128)S(1)}, f32[1,256]{1,0:T(1,128)}, u32[]{:S(2)}) copy-start(f32[1,256]{1,0:T(1,128)} %copy-done.30) | copy-start | bytes 3076
  189.7 20.9 %copy-start.33 = (f32[1,256]{1,0:T(1,128)S(1)}, f32[1,256]{1,0:T(1,128)}, u32[]{:S(2)}) copy-start(f32[1,256]{1,0:T(1,128)} %copy-done.32) | copy-start | bytes 3076
  189.7 20.9 %copy-start.35 = (f32[256]{0:T(256)S(1)}, f32[256]{0:T(256)}, u32[]{:S(2)}) copy-start(f32[256]{0:T(256)} %copy-done.34) | copy-start | bytes 3076
  189.7 20.9 %copy-start.37 = (f32[256]{0:T(256)S(1)}, f32[256]{0:T(256)}, u32[]{:S(2)}) copy-start(f32[256]{0:T(256)} %copy-done.36) | copy-start | bytes 3076
  189.7 20.9 %copy-start.46 = (f32[256]{0:T(256)S(1)}, f32[256]{0:T(256)}, u32[]{:S(2)}) copy-start(f32[256]{0:T(256)} %get-tuple-element.57) | copy-start | bytes 3076
  189.7 20.9 %copy-start.47 = (f32[256]{0:T(256)S(1)}, f32[256]{0:T(256)}, u32[]{:S(2)}) copy-start(f32[256]{0:T(256)} %get-tuple-element.62) | copy-start | bytes 3076
  207.3 4.3 copy-start.11
  207.3 4.2 copy-start.24
  207.4 3.2 collective-permute-start.8
  211.5 3.3 copy-start.22
  211.5 11.7 %copy-start.12 = (bf16[256,1152]{1,0:T(8,128)(2,1)S(1)}, bf16[256,1152]{1,0:T(8,128)(2,1)}, u32[]{:S(2)}) copy-start(bf16[256,1152]{1,0:T(8,128)(2,1)} %get-tuple-element.45) | copy-start | bytes 1769476
  213.0 69.3 %reduce-scatter.11.cloned.1.call-start = ((), (), s32[]{:S(2)}) async-start(), calls=%async_computation.11 | async-start | bytes 655360 | tf_op jit(solution)/shard_map/reduce_scatter | solution.py:126
  214.8 7.7 %collective-permute-start.7 = (bf16[1152,128]{1,0:T(8,128)(2,1)}, bf16[1152,128]{1,0:T(8,128)(2,1)S(1)}, u32[]{:S(2)}, u32[]{:S(2)}) collective-permute-start(bf16[1152,128]{1,0:T(8,128)(2,1)} %collective-permute-done.5), channel_id=1, source_target_pairs={{0,4},{4,8},{8,12},{12,16},{16,20},{20,24},{24,28},{28,0},{1,5},{5... | collective-permute-start | bytes 884744 | tf_op jit(solution)/shard_map/ppermute | solution.py:18
  223.3 3.5 copy-start.7
  223.3 3.5 copy-start.23
  223.3 3.5 copy-start.25
  226.7 77.6 %reduce-scatter.17.cloned.1.call-start = ((), (), s32[]{:S(2)}) async-start(), calls=%async_computation.15 | async-start | bytes 3538944 | tf_op jit(solution)/shard_map/reduce_scatter | solution.py:193
  229.1 1.0 copy-start.3
  229.1 1.2 copy-start.20
  229.1 155.6 %reduce-scatter.21.cloned.1.call-start = ((), (), s32[]{:S(2)}) async-start(), calls=%async_computation.17 | async-start | bytes 10616832 | tf_op jit(solution)/shard_map/reduce_scatter | solution.py:195
  236.4 0.9 copy-start.17
  236.4 2.4 copy-start.10
  236.5 188.3 %reduce-scatter.19.cloned.1.call-start = ((), (), s32[]{:S(2)}) async-start(), calls=%async_computation.16 | async-start | bytes 1179648 | tf_op jit(solution)/shard_map/reduce_scatter | solution.py:194
  238.7 244.4 %reduce-scatter.23.cloned.1.call-start = ((), (), s32[]{:S(2)}) async-start(), calls=%async_computation.18 | async-start | bytes 5308416 | tf_op jit(solution)/shard_map/reduce_scatter | solution.py:196
  241.9 40.3 %copy-start.9 = (f32[64,1024]{1,0:T(8,128)S(1)}, f32[64,1024]{1,0:T(8,128)}, u32[]{:S(2)}) copy-start(f32[64,1024]{1,0:T(8,128)} %reduce-scatter.13.cloned.1.call-done) | copy-start | bytes 786436
  241.9 40.3 %copy-start.40 = (f32[64]{0:T(128)S(1)}, f32[64]{0:T(128)}, u32[]{:S(2)}) copy-start(f32[64]{0:T(128)} %copy-done.38) | copy-start | bytes 772
  242.0 40.3 %copy-start.49 = (f32[64]{0:T(128)S(1)}, f32[64]{0:T(128)}, u32[]{:S(2)}) copy-start(f32[64]{0:T(128)} %copy-done.48) | copy-start | bytes 772
  (6 other events, 4.3 us)
Sparse Core Ops, SparseCore 0:
  9.9 28.3 all-gather.3
  46.6 35.7 reduce-scatter.8
  84.5 37.8 all-gather.5
  124.3 29.3 all-gather.7
  161.3 27.1 reduce-scatter.12
  213.1 20.7 reduce-scatter.14
  236.1 19.9 reduce-scatter.10
  259.5 44.7 reduce-scatter.16
  308.2 76.4 reduce-scatter.20
  388.6 36.0 reduce-scatter.18
  429.1 53.8 reduce-scatter.22
